TPU v7x, 256 devices: a whole 4x4x8 slice. The times are simulated.
256 devices in a mesh: node: 4 (over x), row: 64 (over y, z, core).
Axes of the slice: x: 4, y: 4, z: 8, core: 2. Of those that a mesh axis runs over, the one named last changes fastest.
Arguments:
- front_slab: bfloat16 [8192, 122880], P('node', 'row'), may hold values from -0.046875 to 0.046875
- omega_codes: int32 [122880, 384], P('row'), may hold values from -3 to 3
- block_mask: int32 [32, 192], P('node', 'row'), may hold values 0 or 1
- leaf_pivots: int32 [4, 128], P('node'), may hold values from 0 to 2047, as said below
- mid_pivots: int32 [2, 128], replicated, may hold values from 0 to 255, as said below
- root_pivots: int32 [128], replicated, may hold values from 0 to 255, as said below
Outputs:
- leaf_interp: float32 [8192, 128], P(('node', 'row'))
- mid_interp: float32 [512, 128], P('node')
- root_interp: float32 [256, 128], P('node')
- root_skeleton: float32 [128, 384], replicated
Inputs may be any that keep to these rules, and one draw needn't show every extreme that they name: `leaf_pivots`: each row holds 128 different row numbers of its subtree, 0 and 2047 among them. `mid_pivots`: each row holds 128 different positions among the 256 stacked child skeleton rows, 0 and 255 among them. `root_pivots`: 128 different positions among the 256 stacked middle skeleton rows, 0 and 255 among them.
All inputs are finite; a program needn't handle non-finite values. No bound on the sum of `block_mask` on one device may be relied on, other than what follows from the above.
Results may differ from a plain program's by a relative error of at most 0.0003.
Values sent between devices are 32-bit elements; how exact they have to be, the bound alone decides.
A program may use at most 128 MiB of HBM per device.

v0:
```python
import jax
import jax.numpy as jnp
from jax import lax
from jax.sharding import PartitionSpec as P


def from_partner(block, axis, distance):
    count = lax.axis_size(axis)
    route = []
    for low in range(count):
        high = low | 1 << distance
        if high != low and high < count:
            route += [(low, high), (high, low)]
    return lax.ppermute(block, axis, route)


def interpolate(sample_block, skeleton):
    gram_matrix = jnp.dot(
        skeleton, skeleton.T, precision=lax.Precision.HIGHEST, preferred_element_type=jnp.float32
    )
    factor = jnp.linalg.cholesky(gram_matrix)
    cross_terms = jnp.dot(
        skeleton,
        sample_block.T,
        precision=lax.Precision.HIGHEST,
        preferred_element_type=jnp.float32,
    )
    return jax.scipy.linalg.cho_solve((factor, True), cross_terms).T


def per_device(front_slab, omega_codes, block_mask, leaf_pivots, mid_pivots, root_pivots):
    slab_height, slab_width = front_slab.shape
    samples_count = omega_codes.shape[1]
    skeleton_size = leaf_pivots.shape[1]
    subtree_id = lax.axis_index("node")
    row_place = lax.axis_index("row")
    subtree_count = lax.axis_size("node")
    sketch = omega_codes.astype(jnp.bfloat16) * jnp.bfloat16(0.5)
    mark_rows, mark_cols = block_mask.shape
    masked = (
        front_slab.reshape(mark_rows, slab_height // mark_rows, mark_cols, slab_width // mark_cols)
        * block_mask.astype(jnp.bfloat16)[:, None, :, None]
    ).reshape(slab_height, slab_width)
    columns = row_place * slab_width + lax.iota(jnp.int32, slab_width)
    span_rows = slab_height * subtree_count
    region = jnp.where(columns < span_rows, columns // slab_height, subtree_count)
    groups = lax.iota(jnp.int32, subtree_count + 1)
    off_range = (region != subtree_id).astype(jnp.bfloat16)
    sketch_off = sketch * off_range[:, None]
    picked = jnp.take(masked, leaf_pivots[0], axis=0)
    span_count = min(subtree_count + 1, slab_width // slab_height + 2)
    first_region = region[0]
    range_terms = jnp.zeros((skeleton_size, subtree_count + 1, samples_count), jnp.float32)
    for offset in range(span_count):
        target = first_region + offset
        keep = (region == target).astype(jnp.bfloat16)
        partial_range = jnp.dot(picked * keep[None, :], sketch, preferred_element_type=jnp.float32)
        slot = (groups == target).astype(jnp.float32)
        range_terms = range_terms + partial_range[:, None, :] * slot[None, :, None]
    pivot_terms = range_terms.reshape(skeleton_size, (subtree_count + 1) * samples_count)
    share_rows = slab_height // lax.axis_size("row")
    partials = jnp.dot(masked, sketch_off, preferred_element_type=jnp.float32)
    summed, pivot_sum = lax.psum((partials, pivot_terms), "row")
    sample_block = lax.dynamic_slice_in_dim(summed, row_place * share_rows, share_rows, 0)
    blocks = pivot_sum.reshape(skeleton_size, subtree_count + 1, samples_count)
    leaf_sel = (groups != subtree_id).astype(jnp.float32)
    outer_sel = (groups // 2 != subtree_id // 2).astype(jnp.float32)
    leaf_skeleton = jnp.einsum("kjs,j->ks", blocks, leaf_sel, precision=lax.Precision.HIGHEST)
    leaf_out = interpolate(sample_block, leaf_skeleton)
    outer_pieces = jnp.einsum("kjs,j->ks", blocks, outer_sel, precision=lax.Precision.HIGHEST)
    far_pieces = blocks[:, subtree_count, :]
    parent = subtree_id // 2
    mid_row = lax.dynamic_index_in_dim(mid_pivots, parent, 0, keepdims=False)
    other_outer, other_far = from_partner((outer_pieces, far_pieces), "node", 0)
    first_child = subtree_id % 2 == 0
    stack = jnp.where(
        first_child,
        jnp.concatenate([outer_pieces, other_outer], axis=0),
        jnp.concatenate([other_outer, outer_pieces], axis=0),
    )
    far_stack = jnp.where(
        first_child,
        jnp.concatenate([far_pieces, other_far], axis=0),
        jnp.concatenate([other_far, far_pieces], axis=0),
    )
    upper_rows = jnp.take(far_stack, mid_row, axis=0)
    other_upper = from_partner(upper_rows, "node", 1)
    top_rows = jnp.where(
        parent == 0,
        jnp.concatenate([upper_rows, other_upper], axis=0),
        jnp.concatenate([other_upper, upper_rows], axis=0),
    )
    mid_skeleton = jnp.take(stack, mid_row, axis=0)
    mid_out = interpolate(outer_pieces, mid_skeleton)
    root_skeleton = jnp.take(top_rows, root_pivots, axis=0)
    root_share = 2 * skeleton_size // subtree_count
    root_block = lax.dynamic_slice_in_dim(top_rows, subtree_id * root_share, root_share, 0)
    root_out = interpolate(root_block, root_skeleton)
    return (leaf_out, mid_out, root_out, root_skeleton)


def solution(mesh):
    return jax.shard_map(
        per_device,
        mesh=mesh,
        in_specs=(P("node", "row"), P("row", None), P("node", "row"), P("node", None), P(), P()),
        out_specs=(P(("node", "row"), None), P("node", None), P("node", None), P()),
        check_vma=False,
    )
```

profile of v0, /device:TPU:1, one launch (start us, length us, event | category | flops | bytes accessed | tf_op | source)
XLA Modules:
  0.0 356.9 jit_solution(3081975688286620107)
XLA Ops:
  7.2 0.7 fusion.65
  7.9 0.7 compare_and_fusion.2
  9.7 0.7 compare_convert_fusion
  11.1 0.7 convert_element_type.41
  12.3 6.5 %copy.26 = bf16[240,8,8,256]{3,1,2,0:T(8,128)(2,1)} copy(bf16[240,8,8,256]{3,2,1,0:T(8,128)(2,1)S(1)} %bitcast.86) | data formatting | bytes 15728640
  18.9 10.9 %copy.14 = bf16[2048,1920]{1,0:T(8,128)(2,1)} copy(bf16[2048,1920]{0,1:T(8,128)(2,1)} %bitcast.87) | data formatting | bytes 15728640 | tf_op jit(solution)/shard_map/mul | solution.py:41
  29.7 10.6 %mul.96 = bf16[2048,1920]{1,0:T(8,128)(2,1)} multiply(bf16[2048,1920]{1,0:T(8,128)(2,1)} %param.9, bf16[2048,1920]{1,0:T(8,128)(2,1)} %copy.14) | non-fusion elementwise | flops 3932160 | bytes 23592960 | tf_op jit(solution)/shard_map/mul | solution.py:41
  40.3 5.8 %gather_fusion = bf16[128,1920]{1,0:T(8,128)(2,1)S(1)} fusion(bf16[2048,1920]{1,0:T(8,128)(2,1)} %mul.96, s32[1024]{0:T(1024)S(1)} %pad_clamp_fusion.2), kind=kCustom, calls=%fused_computation.3 | custom fusion | bytes 983552 | tf_op jit(solution)/shard_map/jit(_take)/gather | solution.py:50
  46.2 1.5 fusion.6
  47.7 1.5 fusion.8
  49.3 2.6 fusion.10
  51.8 2.5 copy.17
  54.4 9.4 %fusion.4 = f32[2048,384]{1,0:T(8,128)} fusion(bf16[2048,1920]{1,0:T(8,128)(2,1)} %mul.96, bf16[1920]{0:T(1024)(128)(2,1)S(1)} %compare_select_fusion, s32[1920,384]{1,0:T(8,128)S(1)} %copy-done), kind=kOutput, calls=%fused_computation.8 | convolution fusion | flops 3021373440 | bytes 13963008 | tf_op jit(solution)/shard_map/dot_general | solution.py:62
  64.5 197.3 %all-reduce.3.cloned.1.call-done = (f32[128,5,384]{2,0,1:T(8,128)}, f32[2048,384]{1,0:T(8,128)}) async-done(((f32[128,5,384]{2,0,1:T(8,128)}, f32[2048,384]{1,0:T(8,128)}), (f32[128,5,384]{2,0,1:T(8,128)}, f32[2048,384]{1,0:T(8,128)})) %all-reduce.3.cloned.1.call-update) | async-done | bytes 4128784 | tf_op jit(solution)/shard_map/psum | solution.py:63
  261.8 1.0 slice_bitcast_fusion
  262.8 2.7 fusion
  265.6 1.4 fusion.2
  267.0 1.3 collective-permute-start.1
  269.1 11.7 %cholesky.59 = f32[128,128]{1,0:T(8,128)S(1)} custom-call(f32[128,128]{1,0:T(8,128)S(1)} %fusion.51), custom_call_target="Cholesky" | custom-call | tf_op jit(solution)/shard_map/jit(cholesky)/cholesky | solution.py:21
  282.2 9.8 %custom-call.23 = f32[1,128,128]{1,2,0:T(8,128)S(1)} custom-call(f32[1,128,128]{2,1,0:T(8,128)S(1)} %fusion.34), custom_call_target="InvertDiagBlocksLowerTriangular" | custom-call | tf_op jit(solution)/shard_map/jit(_cho_solve)/triangular_solve | solution.py:28
  292.0 1.1 fusion.18
  293.4 0.9 fusion.47
  294.3 0.8 gather_fusion.1
  296.0 0.8 gather_fusion.2
  296.9 3.0 collective-permute-start.2
  300.0 11.7 %cholesky.70 = f32[128,128]{1,0:T(8,128)S(1)} custom-call(f32[128,128]{1,0:T(8,128)S(1)} %fusion.46), custom_call_target="Cholesky" | custom-call | tf_op jit(solution)/shard_map/jit(cholesky)/cholesky | solution.py:21
  313.0 9.8 %custom-call.24 = f32[1,128,128]{1,2,0:T(8,128)S(1)} custom-call(f32[1,128,128]{2,1,0:T(8,128)S(1)} %fusion.35), custom_call_target="InvertDiagBlocksLowerTriangular" | custom-call | tf_op jit(solution)/shard_map/jit(_cho_solve)/triangular_solve | solution.py:28
  323.1 0.9 fusion.42
  324.1 0.8 gather_fusion.3
  325.5 11.7 %cholesky.81 = f32[128,128]{1,0:T(8,128)S(1)} custom-call(f32[128,128]{1,0:T(8,128)S(1)} %fusion.41), custom_call_target="Cholesky" | custom-call | tf_op jit(solution)/shard_map/jit(cholesky)/cholesky | solution.py:21
  338.5 9.8 %custom-call.25 = f32[1,128,128]{1,2,0:T(8,128)S(1)} custom-call(f32[1,128,128]{2,1,0:T(8,128)S(1)} %fusion.36), custom_call_target="InvertDiagBlocksLowerTriangular" | custom-call | tf_op jit(solution)/shard_map/jit(_cho_solve)/triangular_solve | solution.py:28
  349.0 0.9 fusion.37
  (61 shorter events, 10.4 us)
Async XLA Ops:
  7.2 254.6 %all-reduce.3.cloned.1.call-start = ((), (), s32[]{:S(2)}) async-start(), calls=%async_computation | async-start | bytes 8257536 | tf_op jit(solution)/shard_map/psum | solution.py:63
  40.3 5.8 %copy-start = (s32[1920,384]{1,0:T(8,128)S(1)}, s32[1920,384]{1,0:T(8,128)}, u32[]{:S(2)}) copy-start(s32[1920,384]{1,0:T(8,128)} %param.10) | copy-start | bytes 8847364
  63.7 0.7 copy-start.3
  63.7 0.7 copy-start.4
  261.8 3.8 %copy-start.1 = (f32[128,5,384]{2,0,1:T(8,128)S(1)}, f32[128,5,384]{2,0,1:T(8,128)}, u32[]{:S(2)}) copy-start(f32[128,5,384]{2,0,1:T(8,128)} %get-tuple-element.6) | copy-start | bytes 2949124
  267.0 29.0 %collective-permute-start.1 = (f32[128,384]{1,0:T(8,128)S(1)}, f32[128,384]{1,0:T(8,128)S(1)}, u32[]{:S(2)}, u32[]{:S(2)}) collective-permute-start(f32[128,384]{1,0:T(8,128)S(1)} %slice_bitcast_fusion), channel_id=1, source_target_pairs={{0,64},{64,0},{128,192},{192,128},{1,65},{65,1},{129,193},{193,129... | collective-permute-start | bytes 589832 | tf_op jit(solution)/shard_map/ppermute | solution.py:14
  268.3 26.0 %collective-permute-start = (f32[128,384]{1,0:T(8,128)S(1)}, f32[128,384]{1,0:T(8,128)S(1)}, u32[]{:S(2)}, u32[]{:S(2)}) collective-permute-start(f32[128,384]{1,0:T(8,128)S(1)} %bitcast.89), channel_id=1, source_target_pairs={{0,64},{64,0},{128,192},{192,128},{1,65},{65,1},{129,193},{193,129... | collective-permute-start | bytes 589832 | tf_op jit(solution)/shard_map/ppermute | solution.py:14
  296.9 27.2 %collective-permute-start.2 = (f32[128,384]{1,0:T(8,128)S(1)}, f32[128,384]{1,0:T(8,128)S(1)}, u32[]{:S(2)}, u32[]{:S(2)}) collective-permute-start(f32[128,384]{1,0:T(8,128)S(1)} %broadcast_select_fusion.4), channel_id=1, source_target_pairs={{0,128},{128,0},{64,192},{192,64},{1,129},{129,1},{65,193},{193,65... | collective-permute-start | bytes 589832 | tf_op jit(solution)/shard_map/ppermute | solution.py:14
  324.9 24.9 %copy-start.2 = (f32[128,384]{1,0:T(8,128)}, f32[128,384]{1,0:T(8,128)S(1)}, u32[]{:S(2)}) copy-start(f32[128,384]{1,0:T(8,128)S(1)} %broadcast_select_fusion.3) | copy-start | bytes 589828
Sparse Core Ops, SparseCore 0:
  63.9 197.8 all-reduce.2
where the time goes:
time: 363 us; the launch traced here: 357 us
  waiting for transfers between devices  197 us (54%)
  other arithmetic  85.4 us (24%)
  local copies, waits for them, and re-layouts  31.2 us (9%)
  matrix products  23 us (6%)
  between operations  15.3 us (4%)
  starting transfers between devices  4.67 us (1%)
    psum x1, waiting for transfers between devices, per_device(): summed, pivot_sum = lax.psum((partials, pivot_terms), 'row')  197 us
    another operation x9, other arithmetic, interpolate(): factor = jnp.linalg.cholesky(gram_matrix)  37.2 us
    another operation x6, other arithmetic, interpolate(): return jax.scipy.linalg.cho_solve((factor, True), cross_terms).T  31.4 us
    mul x2, local copies, waits for them, and re-layouts, per_device(): front_slab.reshape(mark_rows, slab_height // mark_rows, mark_cols, slab_w...  11.4 us
    mul x1, other arithmetic, per_device(): front_slab.reshape(mark_rows, slab_height // mark_rows, mark_cols, slab_w...  10.6 us
    dot_general x1, matrix products, per_device(): partials = jnp.dot(masked, sketch_off, preferred_element_type=jnp.float32)  9.37 us
  transfers between devices with their start and end apart: 4, of which 1 were waited for; matrix products, arithmetic and copies ran while one was open for 14% of the time, Pallas kernels for 0%

commit v1 on v0

v1 whole, which is shorter than its diff:
```python
import jax
import jax.numpy as jnp
from jax import lax
from jax.experimental import pallas as pl
from jax.experimental.pallas import tpu as pltpu
from jax.sharding import PartitionSpec as P

F32 = jnp.float32
BF16 = jnp.bfloat16
MESH = pl.DeviceIdType.MESH
TOP = lax.Precision.HIGHEST

NX, NY, NZ, NC = 4, 4, 8, 2
SIDE = 128
SAMPLES = 384
CHUNK = 256
HALF = SAMPLES // NC
PART = HALF // NY


def exact_dot(a, b):
    return jnp.dot(a, b, precision=TOP, preferred_element_type=F32)


def flip(block):
    rows, cols = block.shape
    return jnp.concatenate(
        [
            jnp.concatenate(
                [block[i : i + SIDE, j : j + SIDE].T for i in range(0, rows, SIDE)], axis=1
            )
            for j in range(0, cols, SIDE)
        ],
        axis=0,
    )


def inverses(matrices):
    n, b = SIDE, 8
    lane = lax.broadcasted_iota(jnp.int32, (8, n), 1)
    sub = lax.broadcasted_iota(jnp.int32, (8, n), 0)
    work = [[m[8 * g : 8 * g + 8, :] for g in range(n // 8)] for m in matrices]
    for k in range(0, n, b):
        own = k // 8
        inside = (lane >= k) & (lane < k + b)
        for t, m in enumerate(work):
            col = [
                [jnp.broadcast_to(m[g][:, k + j : k + j + 1], (8, n)) for g in range(n // 8)]
                for j in range(b)
            ]
            row = [jnp.broadcast_to(m[own][j : j + 1, :], (8, n)) for j in range(b)]
            e = [[None] * b for _ in range(b)]
            for i in range(b):
                for j in range(i, b):
                    e[i][j] = jnp.broadcast_to(col[j][own][i : i + 1, :], (8, n))
            u = [jnp.where(inside, jnp.where(lane == k + j, -1.0, 0.0), row[j]) for j in range(b)]
            d = [None] * b
            low = [[None] * b for _ in range(b)]
            for j in range(b):
                d[j] = pltpu.reciprocal(e[j][j], approx=False)
                for i in range(j + 1, b):
                    low[i][j] = e[j][i] * d[j]
                    for q in range(i, b):
                        e[i][q] = e[i][q] - low[i][j] * e[j][q]
                    u[i] = u[i] - low[i][j] * u[j]
            v = [None] * b
            for i in reversed(range(b)):
                v[i] = d[i] * u[i]
                for q in range(i + 1, b):
                    v[i] = v[i] - low[q][i] * v[q]
            new = []
            for g in range(n // 8):
                z = jnp.where(inside, 0.0, m[g])
                if g == own:
                    z = jnp.zeros_like(z)
                for j in range(b):
                    c = col[j][g]
                    if g == own:
                        c = jnp.where(sub == j, -1.0, 0.0)
                    z = z - c * v[j]
                new.append(z)
            work[t] = new
    return [-jnp.concatenate(m, axis=0) for m in work]


def kernel(
    slab_hbm, codes_hbm, marks, leaf_piv, mid_piv, root_piv,
    leaf_out, mid_out, root_out, skel_out,
    slab, codes, omega, tall, tall_in, qt, cb, hb, yb, zb, rz, rzo, fo, st,
    xf, xo, mt, xh, xyb, xz, xzb,
    load_sem, send_sem, recv_sem,
):
    n = lax.axis_index("node")
    r = lax.axis_index("row")
    y, z, c = r // (NZ * NC), (r // NC) % NZ, r % NC
    chunks = slab.shape[0] // CHUNK
    width = slab.shape[1]
    span = slab.shape[0]
    mark_width = width // marks.shape[1]

    def where_is(x_at, y_at, z_at, c_at):
        return (x_at, y_at * (NZ * NC) + z_at * NC + c_at)

    load_omega = pltpu.make_async_copy(codes_hbm, codes, load_sem.at[chunks])
    load_omega.start()
    loads = []
    for a in range(chunks):
        place = pl.ds(a * CHUNK, CHUNK)
        loads.append(
            pltpu.make_async_copy(slab_hbm.at[place], slab.at[place], load_sem.at[a])
        )
        loads[-1].start()

    sibling = where_is(n, y, z, 1 - c)
    on_y = [where_is(n, (y + d) % NY, z, c) for d in range(1, NY)]
    on_z = [where_is(n, y, (z + d) % NZ, c) for d in range(1, NZ)]
    on_x = [where_is((n + d) % NX, y, z, c) for d in range(1, NX)]
    pair = where_is(n + 1 - 2 * (n % 2), y, z, c)
    barrier = pltpu.get_barrier_semaphore()
    friends = [sibling] + on_y + on_z + on_x
    for friend in friends:
        pl.semaphore_signal(barrier, inc=1, device_id=friend, device_id_type=MESH)

    count = [0]
    sent = []

    def remote(src, dst, to):
        at = count[0]
        count[0] += 1
        return pltpu.make_async_remote_copy(
            src_ref=src, dst_ref=dst, send_sem=send_sem.at[at], recv_sem=recv_sem.at[at],
            device_id=to, device_id_type=MESH,
        )

    def go(copy):
        copy.start()
        sent.append(copy)

    lane = lax.broadcasted_iota(jnp.int32, (1, width), 1)
    column = lane + r * width
    region = jnp.where(column < NX * span, column // span, NX)
    off_leaf = (region != n).astype(F32)
    off_outer = (region // 2 != n // 2).astype(F32)
    off_far = (region == NX).astype(F32)
    mark_of = lane // mark_width

    def masked(a):
        keep = jnp.zeros_like(off_leaf)
        for b in range(marks.shape[1]):
            keep = jnp.where(mark_of == b, marks[a, b].astype(F32), keep)
        keep = (keep * off_leaf).astype(BF16)
        return slab[pl.ds(pl.multiple_of(a * CHUNK, CHUNK), CHUNK), :] * keep

    load_omega.wait()
    omega[...] = (codes[...].astype(F32) * 0.5).astype(BF16)
    piv_rows = jnp.broadcast_to(leaf_piv[0:1, :].astype(F32), (SIDE, SIDE)).T.astype(jnp.int32)
    spot = lax.broadcasted_iota(jnp.int32, (SIDE, SIDE), 1)
    picked = jnp.zeros((SIDE, width), F32)
    for a in range(chunks):
        loads[a].wait()
        pick = jnp.concatenate(
            [
                jnp.where(piv_rows == spot + (a * CHUNK + h), 1.0, 0.0)
                for h in range(0, CHUNK, SIDE)
            ],
            axis=1,
        ).astype(BF16)
        picked = picked + jnp.dot(pick, masked(a), preferred_element_type=F32)

    special = z <= 2
    near = special & (y == 0)
    part_l = flip(jnp.dot(picked.astype(BF16), omega[...], preferred_element_type=F32))
    qt[0] = part_l

    @pl.when(special & (y != 0))
    def _():
        qt[1] = part_l
        qt[2] = part_l

    @pl.when(near)
    def _():
        for i, off in ((1, off_outer), (2, off_far)):
            part = jnp.dot((picked * off).astype(BF16), omega[...], preferred_element_type=F32)
            qt[i] = flip(part)

    pl.semaphore_wait(barrier, len(friends))

    away = pl.ds((1 - c) * HALF, HALF)
    mine = pl.ds(c * HALF, HALF)
    c_l = remote(qt.at[0, away], cb.at[0], sibling)
    c_of = remote(qt.at[pl.ds(1, 2), away], cb.at[pl.ds(1, 2)], sibling)
    go(c_l)
    pl.when(special)(c_of.start)

    def tall_chunk(a):
        res = jnp.dot(masked(a), omega[...], preferred_element_type=F32)
        at_y, z0 = a // 2, (a % 2) * (CHUNK // 64)
        for i in range(CHUNK // 32):
            zz, cc = i // 2, i % 2
            rows = pl.ds(pl.multiple_of((z0 + zz) * 32, 32), 32)
            tall[cc, at_y, rows, :] = res[i * 32 : (i + 1) * 32]

    tall_copies = [remote(tall.at[1 - c, q], tall_in.at[q], sibling) for q in range(NY)]

    def tall_part(q):
        tall_chunk(2 * q)
        tall_chunk(2 * q + 1)
        go(tall_copies[q])

    tall_part(0)
    c_l.wait_recv()
    hb[0] = qt[0, mine, :] + cb[0]
    y_l = [remote(hb.at[0, pl.ds((y + d) % NY * PART, PART)], yb.at[d - 1, 0], on_y[d - 1]) for d in range(1, NY)]
    y_of = [
        remote(hb.at[pl.ds(1, 2), pl.ds((y + d) % NY * PART, PART)], yb.at[d - 1, pl.ds(1, 2)], on_y[d - 1])
        for d in range(1, NY)
    ]
    for d in (2, 1, 3):
        go(y_l[d - 1])

    @pl.when(special)
    def _():
        c_of.wait_recv()
        for i in (1, 2):
            hb[i] = qt[i, mine, :] + cb[i]
        for d in (2, 1, 3):
            y_of[d - 1].start()

    for q in range(1, NY):
        tall_part(q)

    own_y = pl.ds(y * PART, PART)
    for d in range(1, NY):
        y_l[d - 1].wait_recv()
    zb[0] = hb[0, own_y, :] + yb[0, 0] + yb[1, 0] + yb[2, 0]
    z_order = (4, 3, 5, 2, 6, 1, 7)
    z_l = [remote(zb.at[0], rz.at[z], on_z[d - 1]) for d in range(1, NZ)]
    z_of = [remote(zb.at[pl.ds(1, 2)], rzo.at[z], on_z[d - 1]) for d in range(1, NZ)]
    for d in z_order:
        go(z_l[d - 1])
    rz[z] = zb[0]

    @pl.when(special)
    def _():
        for d in range(1, NY):
            y_of[d - 1].wait_recv()
        for i in (1, 2):
            zb[i] = hb[i, own_y, :] + yb[0, i] + yb[1, i] + yb[2, i]
        for d in z_order:
            z_of[d - 1].start()
        rzo[z] = zb[1:3]

    for q in range(NY):
        tall_copies[q].wait_recv()
        tall_in[q] = tall_in[q] + tall[c, q]

    for d in range(1, NZ):
        z_l[d - 1].wait_recv()
    total = rz[0]
    for i in range(1, NZ):
        total = total + rz[i]
    here = c * HALF + y * PART
    st[pl.ds(here, PART), :] = total

    def spread(ref_at, sends_y):
        pass

    def st_at(y_at):
        return st.at[pl.ds(c * HALF + y_at * PART, PART)]

    s_y = [remote(st_at(y), st_at(y), on_y[d - 1]) for d in range(1, NY)]
    s_c = [remote(st_at((y + NY - d) % NY), st_at((y + NY - d) % NY), sibling) for d in range(NY)]
    for d in (2, 1, 3):
        go(s_y[d - 1])
    go(s_c[0])

    for i in range(NZ):
        is_special = i <= 2
        if is_special:

            @pl.when(z != i)
            def _():
                for d in range(1, NZ):

                    @pl.when((z + NZ - d) % NZ == i)
                    def _():
                        z_of[d - 1].wait_recv()

    for i in range(2):
        part = rzo[0, i] + rzo[1, i] + rzo[2, i]
        for j in range(3, NZ):
            part = part + rz[j]
        fo[i] = part
    xo[n % 2] = fo[0]
    xf[n] = fo[1]
    x_o = remote(fo.at[0], xo.at[n % 2], pair)
    x_f = [remote(fo.at[1], xf.at[n], on_x[d - 1]) for d in range(1, NX)]
    go(x_f[1])
    go(x_o)
    go(x_f[0])
    go(x_f[2])

    for d in range(1, NY):
        s_y[d - 1].wait_recv()
        go(s_c[d])

    x_o.wait_recv()
    for d in range(1, NX):
        x_f[d - 1].wait_recv()
    from_sub = lax.broadcasted_iota(jnp.int32, (2 * SIDE, SIDE), 0)

    def chooser(row):
        return jnp.where(from_sub == row, 1.0, 0.0)

    parent = n // 2
    choose_mid = [chooser(mid_piv[q : q + 1, :]) for q in range(2)]
    choose_own = jnp.where(parent == 0, choose_mid[0], choose_mid[1])
    upper = [
        exact_dot(jnp.concatenate([xf[2 * q], xf[2 * q + 1]], axis=1), choose_mid[q])
        for q in range(2)
    ]
    own_part = pl.ds(here, PART)
    mt[0, own_part, :] = exact_dot(jnp.concatenate([xo[0], xo[1]], axis=1), choose_own)
    mt[1, own_part, :] = fo[0]
    mt[2, own_part, :] = exact_dot(jnp.concatenate(upper, axis=1), chooser(root_piv[0:1, :]))
    mt[3, own_part, :] = jnp.where(parent == 0, upper[0], upper[1])

    def mt_at(y_at):
        return mt.at[:, pl.ds(c * HALF + y_at * PART, PART)]

    m_y = [remote(mt_at(y), mt_at(y), on_y[d - 1]) for d in range(1, NY)]
    m_c = [remote(mt_at((y + NY - d) % NY), mt_at((y + NY - d) % NY), sibling) for d in range(NY)]
    for d in (2, 1, 3):
        go(m_y[d - 1])
    go(m_c[0])

    for copy in s_c:
        copy.wait_recv()
    skeleton_t = st[...]
    for q in range(NY):
        xh[q] = exact_dot(tall_in[q], skeleton_t)
    l_y = [remote(xh.at[(y + d) % NY], xyb.at[d - 1], on_y[d - 1]) for d in range(1, NY)]
    for d in (2, 1, 3):
        go(l_y[d - 1])

    leaf_inv = inverses([exact_dot(flip(skeleton_t), skeleton_t)])[0]

    for d in range(1, NY):
        m_y[d - 1].wait_recv()
        go(m_c[d])
    for copy in l_y:
        copy.wait_recv()
    xz[...] = xh[y] + xyb[0] + xyb[1] + xyb[2]
    l_z = [remote(xz.at[pl.ds((z + d) % NZ * 32, 32)], xzb.at[d - 1], on_z[d - 1]) for d in range(1, NZ)]
    for d in z_order:
        go(l_z[d - 1])

    for copy in m_c:
        copy.wait_recv()
    mid_t, outer_t, root_t, top_t = (mt[i] for i in range(4))
    root_skeleton = flip(root_t)
    skel_out[...] = root_skeleton
    mid_inv, root_inv = inverses([exact_dot(flip(mid_t), mid_t), exact_dot(root_skeleton, root_t)])
    mid_out[...] = exact_dot(exact_dot(flip(outer_t), mid_t), mid_inv)
    top_all = exact_dot(exact_dot(flip(top_t), root_t), root_inv)
    root_out[...] = jnp.where(n % 2 == 0, top_all[: SIDE // 2], top_all[SIDE // 2 :])

    cross = xz[pl.ds(z * 32, 32), :]
    for d in range(1, NZ):
        l_z[d - 1].wait_recv()
        cross = cross + xzb[d - 1]
    leaf_out[...] = exact_dot(cross, leaf_inv)

    for copy in sent:
        copy.wait_send()

    @pl.when(special)
    def _():
        c_of.wait_send()
        for copy in y_of + z_of:
            copy.wait_send()


COPIES = 80


def per_device(front_slab, omega_codes, block_mask, leaf_pivots, mid_pivots, root_pivots):
    height, width = front_slab.shape
    samples = omega_codes.shape[1]
    vmem = pl.BlockSpec(memory_space=pltpu.VMEM)
    anywhere = pl.BlockSpec(memory_space=pl.ANY)
    share = height // (NY * NZ * NC)
    half = height // NC
    return pl.pallas_call(
        kernel,
        out_shape=(
            jax.ShapeDtypeStruct((share, SIDE), F32),
            jax.ShapeDtypeStruct((SIDE, SIDE), F32),
            jax.ShapeDtypeStruct((SIDE // 2, SIDE), F32),
            jax.ShapeDtypeStruct((SIDE, samples), F32),
        ),
        in_specs=[anywhere, anywhere, pl.BlockSpec(memory_space=pltpu.SMEM), vmem, vmem, vmem],
        out_specs=(vmem,) * 4,
        scratch_shapes=[
            pltpu.VMEM((height, width), BF16),
            pltpu.VMEM((width, samples), jnp.int32),
            pltpu.VMEM((width, samples), BF16),
            pltpu.VMEM((NC, NY, half // NY, samples), F32),
            pltpu.VMEM((NY, half // NY, samples), F32),
            pltpu.VMEM((3, samples, SIDE), F32),
            pltpu.VMEM((3, HALF, SIDE), F32),
            pltpu.VMEM((3, HALF, SIDE), F32),
            pltpu.VMEM((NY - 1, 3, PART, SIDE), F32),
            pltpu.VMEM((3, PART, SIDE), F32),
            pltpu.VMEM((NZ, PART, SIDE), F32),
            pltpu.VMEM((NZ, 2, PART, SIDE), F32),
            pltpu.VMEM((2, PART, SIDE), F32),
            pltpu.VMEM((samples, SIDE), F32),
            pltpu.VMEM((NX, PART, SIDE), F32),
            pltpu.VMEM((2, PART, SIDE), F32),
            pltpu.VMEM((4, samples, SIDE), F32),
            pltpu.VMEM((NY, half // NY, SIDE), F32),
            pltpu.VMEM((NY - 1, half // NY, SIDE), F32),
            pltpu.VMEM((half // NY, SIDE), F32),
            pltpu.VMEM((NZ - 1, share, SIDE), F32),
            pltpu.SemaphoreType.DMA((16,)),
            pltpu.SemaphoreType.DMA((COPIES,)),
            pltpu.SemaphoreType.DMA((COPIES,)),
        ],
        compiler_params=pltpu.CompilerParams(
            collective_id=0, has_side_effects=True, vmem_limit_bytes=56 << 20
        ),
    )(front_slab, omega_codes, block_mask, leaf_pivots, mid_pivots, root_pivots.reshape(1, SIDE))


def solution(mesh):
    return jax.shard_map(
        per_device,
        mesh=mesh,
        in_specs=(P("node", "row"), P("row", None), P("node", "row"), P("node", None), P(), P()),
        out_specs=(P(("node", "row"), None), P("node", None), P("node", None), P()),
        check_vma=False,
    )
```

time: 363 us -> 67.6 us (0.19); the launches traced: 357 us -> 67.3 us
  waiting for transfers between devices: 197 us -> 0 us
  other arithmetic: 85.4 us -> 0 us
  Pallas kernels: 0 us -> 59.5 us
  local copies, waits for them, and re-layouts: 31.2 us -> 7.13 us
  matrix products: 23 us -> 0 us
  between operations: 15.3 us -> 0.64 us
  starting transfers between devices: 4.67 us -> 0 us
    psum x1 -> x0, waiting for transfers between devices: 197 us -> none  [per_device(): summed, pivot_sum = lax.psum((partials, pivot_terms), 'row')]
    another operation x15 -> x0, other arithmetic: 68.6 us -> none  [the longest x9 37.2 us: interpolate(): factor = jnp.linalg.cholesky(gram_matrix)]
    pallas_call x0 -> x1, Pallas kernels: none -> 59.5 us  [per_device(): pl.pallas_call(kernel, out_shape=(jax.ShapeDtypeStruct((share, SIDE), F32...]
    dot_general x11 -> x0, matrix products: 19.5 us -> none  [the longest x1 9.37 us: per_device(): partials = jnp.dot(masked, sketch_off, preferred_element_type=jnp.float32)]
    mul x6 -> x0, local copies, waits for them, and re-layouts: 11.6 us -> none  [the longest x2 11.4 us: per_device(): front_slab.reshape(mark_rows, slab_height // mark_rows, mark_cols, slab_w...]
    mul x2 -> x0, other arithmetic: 10.6 us -> none  [the longest x1 10.6 us: per_device(): front_slab.reshape(mark_rows, slab_height // mark_rows, mark_cols, slab_w...]
    gather x4 -> x0, local copies, waits for them, and re-layouts: 8.1 us -> none  [the longest x1 5.81 us: per_device(): picked = jnp.take(masked, leaf_pivots[0], axis=0)]
    ppermute x3 -> x0, starting transfers between devices: 4.64 us -> none  [from_partner(): return lax.ppermute(block, axis, route)]
  transfers between devices with their start and end apart: 4 -> 0, of which waited for: 1 -> 0; matrix products, arithmetic and copies ran while one was open for 14% -> 0% of each run, Pallas kernels for 0% -> 0%
where the time goes in v1:
time: 67.6 us; the launch traced here: 67.3 us
  Pallas kernels  59.5 us (88%)
  local copies, waits for them, and re-layouts  7.13 us (11%)
    pallas_call x1, Pallas kernels, per_device(): pl.pallas_call(kernel, out_shape=(jax.ShapeDtypeStruct((share, SIDE), F32...  59.5 us
    unnamed x5, local copies, waits for them, and re-layouts  7.13 us

profile of v1, /device:TPU:1, one launch (start us, length us, event | category | flops | bytes accessed | tf_op | source)
XLA Modules:
  0.0 67.3 jit_solution(16180585827711455153)
XLA Ops:
  0.6 1.3 %copy.10.marks = s32[8,3]{1,0:T(8,128)} copy(s32[8,3]{0,1:T(4,128)} %param.8) | data formatting | bytes 192 | tf_op args[2]
  2.0 59.5 %shard_map.93 = (f32[32,128]{1,0:T(8,128)}, f32[128,128]{1,0:T(8,128)}, f32[64,128]{1,0:T(8,128)}, f32[128,384]{1,0:T(8,128)}) custom-call(bf16[2048,1920]{1,0:T(8,128)(2,1)} %slab_hbm.1, s32[1920,384]{1,0:T(8,128)} %codes_hbm.1, s32[8,3]{1,0:T(8,128)} %copy.10.marks, s32[1,128]{1,0:T(1,128)} %leaf_piv.1, s32[2,128]{1,0:T(2,128)} %mid_piv.1, s32[1,128]{1,0:T(1,128)} %bitcast.1), custom_call_target="tpu_custom_call" | custom-call | tf_op jit(solution)/shard_map/pallas_call | solution.py:394
  61.5 1.3 %copy.15 = f32[32,128]{1,0:T(8,128)} copy(f32[32,128]{1,0:T(8,128)} %get-tuple-element.8) | data formatting | bytes 32768
  62.8 1.5 %copy.16 = f32[128,128]{1,0:T(8,128)} copy(f32[128,128]{1,0:T(8,128)} %get-tuple-element.9) | data formatting | bytes 131072
  64.3 1.4 %copy.17 = f32[64,128]{1,0:T(8,128)} copy(f32[64,128]{1,0:T(8,128)} %get-tuple-element.10) | data formatting | bytes 65536
  65.7 1.6 %copy.18 = f32[128,384]{1,0:T(8,128)} copy(f32[128,384]{1,0:T(8,128)} %get-tuple-element.11) | data formatting | bytes 393216

commit v2 on v1

v2 whole, which is shorter than its diff:
```python
import jax
import jax.numpy as jnp
from jax import lax
from jax.experimental import pallas as pl
from jax.experimental.pallas import tpu as pltpu
from jax.sharding import PartitionSpec as P

F32 = jnp.float32
BF16 = jnp.bfloat16
MESH = pl.DeviceIdType.MESH
TOP = lax.Precision.HIGHEST

NX, NY, NZ, NC = 4, 4, 8, 2
SIDE = 128
SAMPLES = 384
CHUNK = 256
HALF = SAMPLES // NC
PART = HALF // NY
SPLIT = 48
PIECE = 16


def exact_dot(a, b):
    return jnp.dot(a, b, precision=TOP, preferred_element_type=F32)


def choose_dot(a, chosen):
    high = a.astype(BF16)
    rest = a - high.astype(F32)
    middle = rest.astype(BF16)
    low = (rest - middle.astype(F32)).astype(BF16)
    return sum(jnp.dot(t, chosen, preferred_element_type=F32) for t in (low, middle, high))


def flip(block):
    rows, cols = block.shape
    return jnp.concatenate(
        [
            jnp.concatenate(
                [block[i : i + SIDE, j : j + SIDE].T for i in range(0, rows, SIDE)], axis=1
            )
            for j in range(0, cols, SIDE)
        ],
        axis=0,
    )


def pivot_rows(rows, k):
    b, n = 8, SIDE
    lane = lax.broadcasted_iota(jnp.int32, (b, n), 1)
    inside = (lane >= k) & (lane < k + b)
    col = [jnp.broadcast_to(rows[:, k + j : k + j + 1], (b, n)) for j in range(b)]
    e = [[None] * b for _ in range(b)]
    for i in range(b):
        for j in range(i, b):
            e[i][j] = jnp.broadcast_to(col[j][i : i + 1, :], (b, n))
    u = [
        jnp.where(
            inside,
            jnp.where(lane == k + j, -1.0, 0.0),
            jnp.broadcast_to(rows[j : j + 1, :], (b, n)),
        )
        for j in range(b)
    ]
    d = [None] * b
    low = [[None] * b for _ in range(b)]
    for j in range(b):
        d[j] = pltpu.reciprocal(e[j][j], approx=False)
        for i in range(j + 1, b):
            low[i][j] = e[j][i] * d[j]
            for q in range(i, b):
                e[i][q] = e[i][q] - low[i][j] * e[j][q]
            u[i] = u[i] - low[i][j] * u[j]
    v = [None] * b
    for i in reversed(range(b)):
        v[i] = d[i] * u[i]
        for q in range(i + 1, b):
            v[i] = v[i] - low[q][i] * v[q]
    return v


def row_groups(matrix):
    return [matrix[8 * g : 8 * g + 8, :] for g in range(SIDE // 8)]


def swept(work):
    return [-jnp.concatenate(m, axis=0) for m in work]


def sweep(work, first, last, by_dot):
    b, n = 8, SIDE
    groups = n // b
    lane = lax.broadcasted_iota(jnp.int32, (b, n), 1)
    sub = lax.broadcasted_iota(jnp.int32, (b, n), 0)
    work = list(work)
    for k in range(first, last, b):
        own = k // b
        inside = (lane >= k) & (lane < k + b)
        pivots = [pivot_rows(m[own], k) for m in work]
        for t, m in enumerate(work):
            v = pivots[t]
            new = [None] * groups
            new[own] = v[0]
            for j in range(1, b):
                new[own] = jnp.where(sub == j, v[j], new[own])
            order = [(own + 1 + q) % groups for q in range(groups - 1)]
            if by_dot:
                update = exact_dot(jnp.concatenate(m, axis=0)[:, k : k + b], new[own])
            for at, g in enumerate(order):
                part = jnp.where(inside, 0.0, m[g])
                if by_dot and at > 0:
                    part = part - update[b * g : b * g + b]
                else:
                    for j in range(b):
                        part = part - jnp.broadcast_to(m[g][:, k + j : k + j + 1], (b, n)) * v[j]
                new[g] = part
            work[t] = new
    return work


def kernel(
    slab_hbm, codes_hbm, marks, leaf_piv, mid_piv, root_piv,
    leaf_out, mid_out, root_out, skel_out,
    slab, codes, omega, tall, tall_in, qt, cb, hb, yb, zb, rz, rzo, fo, st,
    xf, xo, mo, mt, xh, x1_in, x2_in, x1, x2, y1_in, y2_in, kept,
    load_sem, send_sem, recv_sem,
):
    n = lax.axis_index("node")
    r = lax.axis_index("row")
    y, z, c = r // (NZ * NC), (r // NC) % NZ, r % NC
    chunks = slab.shape[0] // CHUNK
    width = slab.shape[1]
    span = slab.shape[0]
    mark_width = width // marks.shape[0]

    def where_is(x_at, y_at, z_at, c_at):
        return (x_at, y_at * (NZ * NC) + z_at * NC + c_at)

    def apart(work):
        pl.when(r >= 0)(work)

    load_omega = pltpu.make_async_copy(codes_hbm, codes, load_sem.at[chunks])
    load_omega.start()
    loads = []
    for a in range(chunks):
        place = pl.ds(a * CHUNK, CHUNK)
        loads.append(
            pltpu.make_async_copy(slab_hbm.at[place], slab.at[place], load_sem.at[a])
        )
        loads[-1].start()

    sibling = where_is(n, y, z, 1 - c)
    on_y = [where_is(n, (y + d) % NY, z, c) for d in range(1, NY)]
    on_z = [where_is(n, y, (z + d) % NZ, c) for d in range(1, NZ)]
    on_x = [where_is((n + d) % NX, y, z, c) for d in range(1, NX)]
    pair = where_is(n + 1 - 2 * (n % 2), y, z, c)
    barrier = pltpu.get_barrier_semaphore()
    friends = [sibling] + on_y + on_z + on_x
    for friend in friends:
        pl.semaphore_signal(barrier, inc=1, device_id=friend, device_id_type=MESH)

    count = [0]
    sent = []

    def remote(src, dst, to):
        at = count[0]
        count[0] += 1
        return pltpu.make_async_remote_copy(
            src_ref=src, dst_ref=dst, send_sem=send_sem.at[at], recv_sem=recv_sem.at[at],
            device_id=to, device_id_type=MESH,
        )

    def go(copy):
        copy.start()
        sent.append(copy)

    lane = lax.broadcasted_iota(jnp.int32, (1, width), 1)
    column = lane + r * width
    region = jnp.where(column < NX * span, column // span, NX)
    off_leaf = (region != n).astype(F32)
    off_outer = (region // 2 != n // 2).astype(F32)
    off_far = (region == NX).astype(F32)
    mark_of = lane // mark_width

    def masked(a):
        keep = jnp.zeros_like(off_leaf)
        for b in range(marks.shape[0]):
            keep = jnp.where(mark_of == b, marks[b, a].astype(F32), keep)
        keep = (keep * off_leaf).astype(BF16)
        return slab[pl.ds(pl.multiple_of(a * CHUNK, CHUNK), CHUNK), :] * keep

    load_omega.wait()
    omega[...] = (codes[...].astype(F32) * 0.5).astype(BF16)
    piv_rows = jnp.broadcast_to(leaf_piv[0:1, :].astype(F32), (SIDE, SIDE)).T.astype(jnp.int32)
    spot = lax.broadcasted_iota(jnp.int32, (SIDE, SIDE), 1)
    picked = jnp.zeros((SIDE, width), F32)
    for a in range(chunks):
        loads[a].wait()
        pick = jnp.concatenate(
            [
                jnp.where(piv_rows == spot + (a * CHUNK + h), 1.0, 0.0)
                for h in range(0, CHUNK, SIDE)
            ],
            axis=1,
        ).astype(BF16)
        picked = picked + jnp.dot(pick, masked(a), preferred_element_type=F32)

    special = z <= 2
    near = special & (y == 0)
    qt[0] = flip(jnp.dot(picked.astype(BF16), omega[...], preferred_element_type=F32))
    pl.semaphore_wait(barrier, len(friends))

    away = pl.ds((1 - c) * HALF, HALF)
    mine = pl.ds(c * HALF, HALF)
    c_l = remote(qt.at[0, away], cb.at[0], sibling)
    c_of = remote(qt.at[pl.ds(1, 2), away], cb.at[pl.ds(1, 2)], sibling)
    go(c_l)

    @pl.when(near)
    def _():
        for i, off in ((1, off_outer), (2, off_far)):
            part = jnp.dot((picked * off).astype(BF16), omega[...], preferred_element_type=F32)
            qt[i] = flip(part)
        c_of.start()

    def tall_chunk(a):
        res = jnp.dot(masked(a), omega[...], preferred_element_type=F32)
        at_y, z0 = a // 2, (a % 2) * (CHUNK // 64)
        for i in range(CHUNK // 32):
            zz, cc = i // 2, i % 2
            rows = pl.ds(pl.multiple_of((z0 + zz) * 32, 32), 32)
            tall[cc, at_y, rows, :] = res[i * 32 : (i + 1) * 32]

    tall_copies = [remote(tall.at[1 - c, q], tall_in.at[q], sibling) for q in range(NY)]

    def tall_part(q):
        @apart
        def _():
            tall_chunk(2 * q)
            tall_chunk(2 * q + 1)

        go(tall_copies[q])

    tall_part(0)
    c_l.wait_recv()
    hb[0] = qt[0, mine, :] + cb[0]
    y_l = [remote(hb.at[0, pl.ds((y + d) % NY * PART, PART)], yb.at[d - 1, 0], on_y[d - 1]) for d in range(1, NY)]
    y_of = [
        remote(hb.at[pl.ds(1, 2), pl.ds((y + d) % NY * PART, PART)], yb.at[d - 1, pl.ds(1, 2)], on_y[d - 1])
        for d in range(1, NY)
    ]
    for d in (2, 1, 3):
        go(y_l[d - 1])

    @pl.when(near)
    def _():
        c_of.wait_recv()
        for i in (1, 2):
            hb[i] = qt[i, mine, :] + cb[i]
        for d in (2, 1, 3):
            y_of[d - 1].start()

    tall_part(1)

    own_y = pl.ds(y * PART, PART)
    for d in range(1, NY):
        y_l[d - 1].wait_recv()
    zb[0] = hb[0, own_y, :] + yb[0, 0] + yb[1, 0] + yb[2, 0]
    z_order = (4, 3, 5, 2, 6, 1, 7)
    z_l = [remote(zb.at[0], rz.at[z], on_z[d - 1]) for d in range(1, NZ)]
    z_of = [remote(zb.at[pl.ds(1, 2)], rzo.at[z], on_z[d - 1]) for d in range(1, NZ)]
    for d in z_order:
        go(z_l[d - 1])
    rz[z] = zb[0]

    @pl.when(near)
    def _():
        for i in (1, 2):
            zb[i] = hb[i, own_y, :] + yb[0, 0] + yb[1, 0] + yb[2, 0]

    for d in range(1, NY):

        @pl.when(special & (y == d))
        def _():
            y_of[d - 1].wait_recv()
            base = hb[0, own_y, :]
            for other in range(1, NY):
                if other != d:
                    base = base + yb[other - 1, 0]
            for i in (1, 2):
                zb[i] = base + yb[d - 1, i]

    @pl.when(special)
    def _():
        for d in z_order:
            z_of[d - 1].start()
        rzo[z] = zb[1:3]

    tall_part(2)
    tall_part(3)

    for d in range(1, NZ):
        z_l[d - 1].wait_recv()
    total = rz[0]
    for i in range(1, NZ):
        total = total + rz[i]
    here = c * HALF + y * PART
    st[pl.ds(here, PART), :] = total

    def rows_of(y_at):
        return pl.ds(c * HALF + y_at * PART, PART)

    def gather(view):
        along = [remote(view(y), view(y), on_y[d - 1]) for d in range(1, NY)]
        across = [remote(view((y + NY - d) % NY), view((y + NY - d) % NY), sibling) for d in range(NY)]
        return along, across

    def begin(along, across):
        for d in (2, 1, 3):
            go(along[d - 1])
        go(across[0])

    def forward(along, across):
        for d in range(1, NY):
            along[d - 1].wait_recv()
            go(across[d])

    s_y, s_c = gather(lambda y_at: st.at[rows_of(y_at)])
    begin(s_y, s_c)

    for q in range(NY):
        tall_copies[q].wait_recv()
        tall_in[q] = tall_in[q] + tall[c, q]

    forward(s_y, s_c)
    for copy in s_c:
        copy.wait_recv()
    skeleton_t = st[...]
    first_y = [remote(xh.at[0, (y + d) % NY], x1_in.at[d - 1], on_y[d - 1]) for d in range(1, NY)]
    first_z = [remote(xh.at[1, :, (z + d) % NZ], x2_in.at[d - 1], on_z[d - 1]) for d in range(1, NZ)]
    for d in (2, 1, 3, 0):
        at_y = (y + d) % NY
        cross = exact_dot(tall_in[at_y], skeleton_t)
        for i in range(NZ * 2):
            xh[i % 2, at_y, i // 2] = cross[i * PIECE : (i + 1) * PIECE]
        if d:
            go(first_y[d - 1])

    for i in range(3):

        @pl.when(z != i)
        def _():
            for d in range(1, NZ):

                @pl.when((z + NZ - d) % NZ == i)
                def _():
                    z_of[d - 1].wait_recv()

    for i in range(2):
        part = rzo[0, i] + rzo[1, i] + rzo[2, i]
        for j in range(3, NZ):
            part = part + rz[j]
        fo[i] = part
    xo[n % 2] = fo[0]
    xf[n] = fo[1]
    x_o = remote(fo.at[0], xo.at[n % 2], pair)
    x_f = [remote(fo.at[1], xf.at[n], on_x[d - 1]) for d in range(1, NX)]
    go(x_f[1])
    go(x_o)
    go(x_f[0])
    go(x_f[2])
    for d in z_order:
        go(first_z[d - 1])
    own_part = pl.ds(here, PART)
    mo[own_part, :] = fo[0]
    o_y, o_c = gather(lambda y_at: mo.at[rows_of(y_at)])
    begin(o_y, o_c)

    from_sub = lax.broadcasted_iota(jnp.int32, (2 * SIDE, SIDE), 0)

    def chooser(row):
        return jnp.where(from_sub == row, 1.0, 0.0).astype(BF16)

    parent = n // 2
    choose_mid = [chooser(mid_piv[q : q + 1, :]) for q in range(2)]
    choose_own = jnp.where(parent == 0, choose_mid[0], choose_mid[1])
    @apart
    def _():
        work = [row_groups(exact_dot(flip(st[...]), st[...]))]
        kept[...] = jnp.concatenate(sweep(work, 0, SPLIT, False)[0], axis=0)

    x_o.wait_recv()
    for d in range(1, NX):
        x_f[d - 1].wait_recv()
    upper = [
        choose_dot(jnp.concatenate([xf[2 * q], xf[2 * q + 1]], axis=1), choose_mid[q])
        for q in range(2)
    ]
    mt[0, own_part, :] = choose_dot(jnp.concatenate([xo[0], xo[1]], axis=1), choose_own)
    mt[1, own_part, :] = choose_dot(jnp.concatenate(upper, axis=1), chooser(root_piv[0:1, :]))
    mt[2, own_part, :] = jnp.where(parent == 0, upper[0], upper[1])
    m_y, m_c = gather(lambda y_at: mt.at[:, rows_of(y_at)])
    begin(m_y, m_c)
    forward(o_y, o_c)

    @apart
    def _():
        kept[...] = swept(sweep([row_groups(kept[...])], SPLIT, SIDE, False))[0]


    for copy in first_y:
        copy.wait_recv()
    x1[...] = xh[0, y] + x1_in[0] + x1_in[1] + x1_in[2]
    then_z = [remote(x1.at[(z + d) % NZ], y1_in.at[d - 1], on_z[d - 1]) for d in range(1, NZ)]
    for d in z_order:
        go(then_z[d - 1])

    forward(m_y, m_c)
    for copy in first_z:
        copy.wait_recv()
    total2 = xh[1, :, z]
    for d in range(1, NZ):
        total2 = total2 + x2_in[d - 1]
    x2[...] = total2
    then_y = [remote(x2.at[(y + d) % NY], y2_in.at[d - 1], on_y[d - 1]) for d in range(1, NY)]
    for d in (2, 1, 3):
        go(then_y[d - 1])
    for copy in o_c + m_c:
        copy.wait_recv()
    mid_t, root_t, top_t = (mt[i] for i in range(3))
    outer_t = mo[...]
    root_skeleton = flip(root_t)
    skel_out[...] = root_skeleton
    grams = [exact_dot(flip(mid_t), mid_t), exact_dot(root_skeleton, root_t)]
    mid_inv, root_inv = swept(sweep([row_groups(g) for g in grams], 0, SIDE, True))
    mid_out[...] = exact_dot(exact_dot(flip(outer_t), mid_t), mid_inv)
    top_all = exact_dot(exact_dot(flip(top_t), root_t), root_inv)
    root_out[...] = jnp.where(n % 2 == 0, top_all[: SIDE // 2], top_all[SIDE // 2 :])

    half1 = x1[z]
    for copy, part in zip(then_z, range(NZ - 1)):
        copy.wait_recv()
        half1 = half1 + y1_in[part]
    half2 = x2[y]
    for copy, part in zip(then_y, range(NY - 1)):
        copy.wait_recv()
        half2 = half2 + y2_in[part]
    leaf_out[...] = exact_dot(jnp.concatenate([half1, half2], axis=0), kept[...])

    for copy in sent:
        copy.wait_send()

    @pl.when(near)
    def _():
        c_of.wait_send()
        for copy in y_of:
            copy.wait_send()

    @pl.when(special)
    def _():
        for copy in z_of:
            copy.wait_send()


COPIES = 96


def hand_over(*refs):
    count = len(refs) // 2
    for i in range(count):
        refs[count + i][...] = refs[i][...]


def per_device(front_slab, omega_codes, block_mask, leaf_pivots, mid_pivots, root_pivots):
    height, width = front_slab.shape
    samples = omega_codes.shape[1]
    vmem = pl.BlockSpec(memory_space=pltpu.VMEM)
    anywhere = pl.BlockSpec(memory_space=pl.ANY)
    share = height // (NY * NZ * NC)
    half = height // NC
    results = pl.pallas_call(
        kernel,
        out_shape=(
            jax.ShapeDtypeStruct((share, SIDE), F32),
            jax.ShapeDtypeStruct((SIDE, SIDE), F32),
            jax.ShapeDtypeStruct((SIDE // 2, SIDE), F32),
            jax.ShapeDtypeStruct((SIDE, samples), F32),
        ),
        in_specs=[anywhere, anywhere, pl.BlockSpec(memory_space=pltpu.SMEM), vmem, vmem, vmem],
        out_specs=(vmem,) * 4,
        scratch_shapes=[
            pltpu.VMEM((height, width), BF16),
            pltpu.VMEM((width, samples), jnp.int32),
            pltpu.VMEM((width, samples), BF16),
            pltpu.VMEM((NC, NY, half // NY, samples), F32),
            pltpu.VMEM((NY, half // NY, samples), F32),
            pltpu.VMEM((3, samples, SIDE), F32),
            pltpu.VMEM((3, HALF, SIDE), F32),
            pltpu.VMEM((3, HALF, SIDE), F32),
            pltpu.VMEM((NY - 1, 3, PART, SIDE), F32),
            pltpu.VMEM((3, PART, SIDE), F32),
            pltpu.VMEM((NZ, PART, SIDE), F32),
            pltpu.VMEM((NZ, 2, PART, SIDE), F32),
            pltpu.VMEM((2, PART, SIDE), F32),
            pltpu.VMEM((samples, SIDE), F32),
            pltpu.VMEM((NX, PART, SIDE), F32),
            pltpu.VMEM((2, PART, SIDE), F32),
            pltpu.VMEM((samples, SIDE), F32),
            pltpu.VMEM((3, samples, SIDE), F32),
            pltpu.VMEM((2, NY, NZ, PIECE, SIDE), F32),
            pltpu.VMEM((NY - 1, NZ, PIECE, SIDE), F32),
            pltpu.VMEM((NZ - 1, NY, PIECE, SIDE), F32),
            pltpu.VMEM((NZ, PIECE, SIDE), F32),
            pltpu.VMEM((NY, PIECE, SIDE), F32),
            pltpu.VMEM((NZ - 1, PIECE, SIDE), F32),
            pltpu.VMEM((NY - 1, PIECE, SIDE), F32),
            pltpu.VMEM((SIDE, SIDE), F32),
            pltpu.SemaphoreType.DMA((16,)),
            pltpu.SemaphoreType.DMA((COPIES,)),
            pltpu.SemaphoreType.DMA((COPIES,)),
        ],
        compiler_params=pltpu.CompilerParams(
            collective_id=0, has_side_effects=True, vmem_limit_bytes=56 << 20
        ),
    )(front_slab, omega_codes, block_mask.T, leaf_pivots, mid_pivots, root_pivots.reshape(1, SIDE))
    return pl.pallas_call(
        hand_over,
        out_shape=tuple(jax.ShapeDtypeStruct(v.shape, v.dtype) for v in results),
        in_specs=[vmem] * len(results),
        out_specs=(vmem,) * len(results),
        compiler_params=pltpu.CompilerParams(vmem_limit_bytes=56 << 20),
    )(*results)


def solution(mesh):
    return jax.shard_map(
        per_device,
        mesh=mesh,
        in_specs=(P("node", "row"), P("row", None), P("node", "row"), P("node", None), P(), P()),
        out_specs=(P(("node", "row"), None), P("node", None), P("node", None), P()),
        check_vma=False,
    )
```

time: 67.6 us -> 54.1 us (0.80)
  local copies, waits for them, and re-layouts: 7.13 us -> 0 us
  Pallas kernels: 59.5 us -> 53.4 us
    pallas_call x1, Pallas kernels: 59.5 us -> 51.6 us  [per_device(): pl.pallas_call(kernel, out_shape=(jax.ShapeDtypeStruct((share, SIDE), F32...]
    unnamed x5 -> x0, local copies, waits for them, and re-layouts: 7.13 us -> none
    pallas_call x0 -> x1, Pallas kernels: none -> 1.73 us  [per_device(): pl.pallas_call(hand_over, out_shape=tuple((jax.ShapeDtypeStruct(v.shape,...]
where the time goes in v2:
time: 54.1 us; the launch traced here: 54 us
  Pallas kernels  53.4 us (99%)
  between operations  0.64 us (1%)
    pallas_call x1, Pallas kernels, per_device(): pl.pallas_call(kernel, out_shape=(jax.ShapeDtypeStruct((share, SIDE), F32...  51.6 us
    pallas_call x1, Pallas kernels, per_device(): pl.pallas_call(hand_over, out_shape=tuple((jax.ShapeDtypeStruct(v.shape,...  1.73 us

profile of v2, /device:TPU:1, one launch (start us, length us, event | category | flops | bytes accessed | tf_op | source)
XLA Modules:
  0.0 54.0 jit_solution(4004785298640339605)
XLA Ops:
  0.6 51.6 %shard_map.93 = (f32[32,128]{1,0:T(8,128)}, f32[128,128]{1,0:T(8,128)}, f32[64,128]{1,0:T(8,128)}, f32[128,384]{1,0:T(8,128)}) custom-call(bf16[2048,1920]{1,0:T(8,128)(2,1)} %slab_hbm.1, s32[1920,384]{1,0:T(8,128)} %codes_hbm.1, s32[3,8]{1,0:T(4,128)} %bitcast.2, s32[1,128]{1,0:T(1,128)} %leaf_piv.1, s32[2,128]{1,0:T(2,128)} %mid_piv.1, s32[1,128]{1,0:T(1,128)} %bitcast.3), custom_call_target="tpu_custom_call" | custom-call | tf_op jit(solution)/shard_map/pallas_call | solution.py:481
  52.3 1.7 %shard_map.94 = (f32[32,128]{1,0:T(8,128)}, f32[128,128]{1,0:T(8,128)}, f32[64,128]{1,0:T(8,128)}, f32[128,384]{1,0:T(8,128)}) custom-call(f32[32,128]{1,0:T(8,128)} %get-tuple-element.8.refs_0_, f32[128,128]{1,0:T(8,128)} %get-tuple-element.9.refs_1_, f32[64,128]{1,0:T(8,128)} %get-tuple-element.10.refs_2_, f32[128,384]{1,0:T(8,128)} %get-tuple-element.11.refs_3_), custom_call_target="tpu_custom_call" | custom-call | tf_op jit(solution)/shard_map/pallas_call | solution.py:526

commit v3 on v2

--- a/solution.py
+++ b/solution.py
@@ -16,7 +16,7 @@
 CHUNK = 256
 HALF = SAMPLES // NC
 PART = HALF // NY
-SPLIT = 48
+SPLIT = 0
 PIECE = 16
 
 
@@ -332,6 +332,34 @@
         tall_copies[q].wait_recv()
         tall_in[q] = tall_in[q] + tall[c, q]
 
+    for i in range(3):
+
+        @pl.when(z != i)
+        def _():
+            for d in range(1, NZ):
+
+                @pl.when((z + NZ - d) % NZ == i)
+                def _():
+                    z_of[d - 1].wait_recv()
+
+    for i in range(2):
+        part = rzo[0, i] + rzo[1, i] + rzo[2, i]
+        for j in range(3, NZ):
+            part = part + rz[j]
+        fo[i] = part
+    xo[n % 2] = fo[0]
+    xf[n] = fo[1]
+    x_o = remote(fo.at[0], xo.at[n % 2], pair)
+    x_f = [remote(fo.at[1], xf.at[n], on_x[d - 1]) for d in range(1, NX)]
+    go(x_f[1])
+    go(x_o)
+    go(x_f[0])
+    go(x_f[2])
+    own_part = pl.ds(here, PART)
+    mo[own_part, :] = fo[0]
+    o_y, o_c = gather(lambda y_at: mo.at[rows_of(y_at)])
+    begin(o_y, o_c)
+
     forward(s_y, s_c)
     for copy in s_c:
         copy.wait_recv()
@@ -345,36 +373,8 @@
             xh[i % 2, at_y, i // 2] = cross[i * PIECE : (i + 1) * PIECE]
         if d:
             go(first_y[d - 1])
-
-    for i in range(3):
-
-        @pl.when(z != i)
-        def _():
-            for d in range(1, NZ):
-
-                @pl.when((z + NZ - d) % NZ == i)
-                def _():
-                    z_of[d - 1].wait_recv()
-
-    for i in range(2):
-        part = rzo[0, i] + rzo[1, i] + rzo[2, i]
-        for j in range(3, NZ):
-            part = part + rz[j]
-        fo[i] = part
-    xo[n % 2] = fo[0]
-    xf[n] = fo[1]
-    x_o = remote(fo.at[0], xo.at[n % 2], pair)
-    x_f = [remote(fo.at[1], xf.at[n], on_x[d - 1]) for d in range(1, NX)]
-    go(x_f[1])
-    go(x_o)
-    go(x_f[0])
-    go(x_f[2])
     for d in z_order:
         go(first_z[d - 1])
-    own_part = pl.ds(here, PART)
-    mo[own_part, :] = fo[0]
-    o_y, o_c = gather(lambda y_at: mo.at[rows_of(y_at)])
-    begin(o_y, o_c)
 
     from_sub = lax.broadcasted_iota(jnp.int32, (2 * SIDE, SIDE), 0)
 

time: 54.1 us -> 51.7 us (0.956)
  Pallas kernels: 53.4 us -> 50.9 us
    pallas_call x1, Pallas kernels: 51.6 us -> 49.2 us  [per_device(): pl.pallas_call(kernel, out_shape=(jax.ShapeDtypeStruct((share, SIDE), F32...]
where the time goes in v3:
time: 51.7 us; the launch traced here: 51.6 us
  Pallas kernels  50.9 us (98%)
  between operations  0.64 us (1%)
    pallas_call x1, Pallas kernels, per_device(): pl.pallas_call(kernel, out_shape=(jax.ShapeDtypeStruct((share, SIDE), F32...  49.2 us
    pallas_call x1, Pallas kernels, per_device(): pl.pallas_call(hand_over, out_shape=tuple((jax.ShapeDtypeStruct(v.shape,...  1.73 us

profile of v3, /device:TPU:1, one launch (start us, length us, event | category | flops | bytes accessed | tf_op | source)
XLA Modules:
  0.0 51.6 jit_solution(12488248081848143244)
XLA Ops:
  0.6 49.2 %shard_map.93 = (f32[32,128]{1,0:T(8,128)}, f32[128,128]{1,0:T(8,128)}, f32[64,128]{1,0:T(8,128)}, f32[128,384]{1,0:T(8,128)}) custom-call(bf16[2048,1920]{1,0:T(8,128)(2,1)} %slab_hbm.1, s32[1920,384]{1,0:T(8,128)} %codes_hbm.1, s32[3,8]{1,0:T(4,128)} %bitcast.2, s32[1,128]{1,0:T(1,128)} %leaf_piv.1, s32[2,128]{1,0:T(2,128)} %mid_piv.1, s32[1,128]{1,0:T(1,128)} %bitcast.3), custom_call_target="tpu_custom_call" | custom-call | tf_op jit(solution)/shard_map/pallas_call | solution.py:481
  49.8 1.7 %shard_map.94 = (f32[32,128]{1,0:T(8,128)}, f32[128,128]{1,0:T(8,128)}, f32[64,128]{1,0:T(8,128)}, f32[128,384]{1,0:T(8,128)}) custom-call(f32[32,128]{1,0:T(8,128)} %get-tuple-element.8.refs_0_, f32[128,128]{1,0:T(8,128)} %get-tuple-element.9.refs_1_, f32[64,128]{1,0:T(8,128)} %get-tuple-element.10.refs_2_, f32[128,384]{1,0:T(8,128)} %get-tuple-element.11.refs_3_), custom_call_target="tpu_custom_call" | custom-call | tf_op jit(solution)/shard_map/pallas_call | solution.py:526

commit v4 on v3

--- a/solution.py
+++ b/solution.py
@@ -408,6 +408,7 @@
         kept[...] = swept(sweep([row_groups(kept[...])], SPLIT, SIDE, False))[0]
 
 
+    forward(m_y, m_c)
     for copy in first_y:
         copy.wait_recv()
     x1[...] = xh[0, y] + x1_in[0] + x1_in[1] + x1_in[2]
@@ -415,7 +416,6 @@
     for d in z_order:
         go(then_z[d - 1])
 
-    forward(m_y, m_c)
     for copy in first_z:
         copy.wait_recv()
     total2 = xh[1, :, z]

time: 51.7 us -> 51.7 us (level)
  no operation moved by 1% of the time
where the time goes in v4:
time: 51.7 us; the launch traced here: 51.6 us
  Pallas kernels  50.9 us (98%)
  between operations  0.64 us (1%)
    pallas_call x1, Pallas kernels, per_device(): pl.pallas_call(kernel, out_shape=(jax.ShapeDtypeStruct((share, SIDE), F32...  49.2 us
    pallas_call x1, Pallas kernels, per_device(): pl.pallas_call(hand_over, out_shape=tuple((jax.ShapeDtypeStruct(v.shape,...  1.73 us

profile of v4, /device:TPU:1, one launch (start us, length us, event | category | flops | bytes accessed | tf_op | source)
XLA Modules:
  0.0 51.6 jit_solution(10030710082986772943)
XLA Ops:
  0.6 49.2 %shard_map.93 = (f32[32,128]{1,0:T(8,128)}, f32[128,128]{1,0:T(8,128)}, f32[64,128]{1,0:T(8,128)}, f32[128,384]{1,0:T(8,128)}) custom-call(bf16[2048,1920]{1,0:T(8,128)(2,1)} %slab_hbm.1, s32[1920,384]{1,0:T(8,128)} %codes_hbm.1, s32[3,8]{1,0:T(4,128)} %bitcast.2, s32[1,128]{1,0:T(1,128)} %leaf_piv.1, s32[2,128]{1,0:T(2,128)} %mid_piv.1, s32[1,128]{1,0:T(1,128)} %bitcast.3), custom_call_target="tpu_custom_call" | custom-call | tf_op jit(solution)/shard_map/pallas_call | solution.py:481
  49.8 1.7 %shard_map.94 = (f32[32,128]{1,0:T(8,128)}, f32[128,128]{1,0:T(8,128)}, f32[64,128]{1,0:T(8,128)}, f32[128,384]{1,0:T(8,128)}) custom-call(f32[32,128]{1,0:T(8,128)} %get-tuple-element.8.refs_0_, f32[128,128]{1,0:T(8,128)} %get-tuple-element.9.refs_1_, f32[64,128]{1,0:T(8,128)} %get-tuple-element.10.refs_2_, f32[128,384]{1,0:T(8,128)} %get-tuple-element.11.refs_3_), custom_call_target="tpu_custom_call" | custom-call | tf_op jit(solution)/shard_map/pallas_call | solution.py:526
